TPU v7x, 32 devices: a whole 2x2x4 slice. The times are simulated.
32 devices in a mesh: row: 4 (over y, x), col: 4 (over z), rep: 2 (over core).
Axes of the slice: x: 2, y: 2, z: 4, core: 2. Of those that a mesh axis runs over, the one named last changes fastest.
Arguments:
- features: bfloat16 [2, 2048, 512], P('rep', ('row', 'col')), may hold values from -6 to 6
- cotangent: bfloat16 [2, 2048, 512], P('rep', ('row', 'col')), may hold values from -6 to 6
- weight: bfloat16 [512, 512], replicated, may hold values from -0.25 to 0.25
- tile_values: bfloat16 [2, 256, 128, 128], P('rep', ('row', 'col')), may hold values from -0.25 to 0.25
- tile_out: int32 [2, 256], P('rep', ('row', 'col')), may hold values from 0 to 3
- tile_in: int32 [2, 256], P('rep', ('row', 'col')), may hold values from 0 to 3
- tile_count: int32 [2, 16], P('rep', ('row', 'col')), may hold values from 8 to 16, as said below
Outputs:
- out_feats: bfloat16 [2, 2048, 512], P('rep', ('row', 'col'))
- grad_feats: bfloat16 [2, 2048, 512], P('rep', ('row', 'col'))
- grad_weight: float32 [512, 512], replicated
Inputs may be any that keep to these rules, and one draw needn't show every extreme that they name: `tile_count`: in each window some group has all 16 slots live.
All inputs are finite; a program needn't handle non-finite values.
Results may differ from a plain program's by a relative error of at most 0.015.
Values may be sent and summed in bfloat16 or wider, within the bound.
A program may use at most 64 MiB of HBM per device.

v0:
```python
import jax
import jax.numpy as jnp
from jax import lax
from jax.sharding import PartitionSpec as P

SECTIONS = 4


def passed_along(value, axis, steps):
    count = lax.axis_size(axis)
    leading, last = (max(0, -steps), min(count, count - steps))
    return lax.ppermute(value, axis, [(source, source + steps) for source in range(leading, last)])


def body(features, cotangent, weight, tile_values, tile_out, tile_in, tile_count):
    field_in = features[0]
    values = tile_values[0]
    outs_idx = tile_out[0]
    ins_idx = tile_in[0]
    count = tile_count[0, 0]
    node_rows, width = field_in.shape
    edge = values.shape[-1]
    per_span = node_rows // edge
    half = SECTIONS // 2
    col_count = lax.axis_size("col")
    out_count = col_count * per_span
    in_count = SECTIONS * per_span
    slot_total = values.shape[0]
    live = (jnp.arange(slot_total, dtype=jnp.int32) < count).astype(jnp.float32)
    out_hot = (outs_idx[None, :] == jnp.arange(out_count, dtype=jnp.int32)[:, None]).astype(
        jnp.float32
    ) * live[None, :]
    in_hot = (ins_idx[None, :] == jnp.arange(in_count, dtype=jnp.int32)[:, None]).astype(
        jnp.float32
    ) * live[None, :]
    pieces = []
    for section in range(SECTIONS):
        offset = section - half
        if offset == 0:
            pieces.append(field_in)
        else:
            pieces.append(passed_along(field_in, "row", -offset))
    blocks = jnp.stack(pieces)
    picked = blocks[ins_idx]
    prods = jnp.einsum("tij,tjf->tif", values, picked, preferred_element_type=jnp.float32)
    part = jnp.einsum("ot,tif->oif", out_hot, prods, precision=lax.Precision.HIGHEST)
    summed = lax.psum_scatter(
        part.reshape(out_count * edge, width).astype(jnp.bfloat16),
        "col",
        scatter_dimension=0,
        tiled=True,
    )
    pre = jnp.dot(summed, weight, preferred_element_type=jnp.float32)
    out_feats = jax.nn.silu(pre).astype(jnp.bfloat16)
    sigma = jax.nn.sigmoid(pre)
    dpre = (cotangent[0].astype(jnp.float32) * sigma * (1.0 + pre * (1.0 - sigma))).astype(
        jnp.bfloat16
    )
    local_grad = jnp.einsum("nf,ng->fg", summed, dpre, preferred_element_type=jnp.float32)
    total_nodes = node_rows * lax.axis_size("row") * col_count * lax.axis_size("rep")
    grad_weight = lax.psum(local_grad, ("row", "col", "rep")) * jnp.float32(total_nodes) ** (-0.5)
    dhidden = jnp.einsum("nf,gf->ng", dpre, weight, preferred_element_type=jnp.float32).astype(
        jnp.bfloat16
    )
    row_grads = lax.all_gather(dhidden, "col", axis=0, tiled=True).reshape(out_count, edge, width)
    chosen = row_grads[outs_idx]
    back_prods = jnp.einsum("tij,tif->tjf", values, chosen, preferred_element_type=jnp.float32)
    sections_part = jnp.einsum("it,tjf->ijf", in_hot, back_prods, precision=lax.Precision.HIGHEST)
    sections_part = sections_part.astype(jnp.bfloat16)
    total = jnp.zeros((node_rows, width), jnp.float32)
    for section in range(SECTIONS):
        offset = section - half
        if offset == 0:
            arrived = sections_part[section]
        else:
            arrived = passed_along(sections_part[section], "row", offset)
        total = total + arrived.astype(jnp.float32)
    grad_feats = total.astype(jnp.bfloat16)
    return (out_feats[None], grad_feats[None], grad_weight)


def solution(mesh):
    return jax.shard_map(
        body,
        mesh=mesh,
        in_specs=(
            P("rep", ("row", "col"), None),
            P("rep", ("row", "col"), None),
            P(),
            P("rep", ("row", "col"), None, None),
            P("rep", ("row", "col")),
            P("rep", ("row", "col")),
            P("rep", ("row", "col")),
        ),
        out_specs=(P("rep", ("row", "col"), None), P("rep", ("row", "col"), None), P()),
        check_vma=False,
    )
```

profile of v0, /device:TPU:0, one launch (start us, length us, event | category | flops | bytes accessed | tf_op | source)
XLA Modules:
  0.0 224.5 jit_solution(10835809086337116893)
XLA Ops:
  7.2 5.0 %collective-permute-start = (bf16[128,512]{1,0:T(8,128)(2,1)}, bf16[128,512]{1,0:T(8,128)(2,1)S(1)}, u32[]{:S(2)}, u32[]{:S(2)}) collective-permute-start(bf16[128,512]{1,0:T(8,128)(2,1)} %bitcast.76), channel_id=1, source_target_pairs={{0,16},{8,24},{1,17},{9,25},{2,18},{10,26},{3,19},{11,27},{4,20},{... | collective-permute-start | bytes 393224 | tf_op jit(solution)/shard_map/ppermute | solution.py:12
  12.2 3.4 %collective-permute-start.1 = (bf16[128,512]{1,0:T(8,128)(2,1)}, bf16[128,512]{1,0:T(8,128)(2,1)S(1)}, u32[]{:S(2)}, u32[]{:S(2)}) collective-permute-start(bf16[128,512]{1,0:T(8,128)(2,1)} %bitcast.77), channel_id=1, source_target_pairs={{0,8},{8,16},{16,24},{1,9},{9,17},{17,25},{2,10},{10,18},{18,26},{... | collective-permute-start | bytes 393224 | tf_op jit(solution)/shard_map/ppermute | solution.py:12
  15.7 1.3 collective-permute-start.2
  18.5 4.3 %collective-permute-done.2 = bf16[128,512]{1,0:T(8,128)(2,1)S(1)} collective-permute-done((bf16[128,512]{1,0:T(8,128)(2,1)}, bf16[128,512]{1,0:T(8,128)(2,1)S(1)}, u32[]{:S(2)}, u32[]{:S(2)}) %collective-permute-start.2) | collective-permute-done | bytes 131104 | tf_op jit(solution)/shard_map/ppermute | solution.py:12
  22.7 1.0 pad_maximum_fusion
  24.4 2.7 %fusion.12 = f32[16,512,128]{2,1,0:T(8,128)} fusion(bf16[16,128,512]{2,1,0:T(8,128)(2,1)S(1)} %gather_fusion, bf16[1,16,128,128]{3,2,1,0:T(8,128)(2,1)S(1)} %copy-done), kind=kOutput, calls=%fused_computation.12 | convolution fusion | flops 268435456 | bytes 6815744 | tf_op jit(solution)/shard_map/tij,tjf->tif/dot_general | solution.py:45
  27.1 5.5 %copy.16 = f32[16,512,128]{1,0,2:T(8,128)} copy(f32[16,512,128]{2,1,0:T(8,128)} %fusion.12) | data formatting | bytes 8388608 | tf_op jit(solution)/shard_map/tij,tjf->tif/dot_general | solution.py:45
  32.6 4.3 %fusion.4 = bf16[4,128,512]{2,0,1:T(4,128)(2,1)S(1)} fusion(f32[16,512,128]{1,0,2:T(8,128)} %copy.16, f32[16]{0:T(128)S(1)} %compare_convert_fusion, s32[16]{0:T(128)S(1)} %bitcast.82), kind=kOutput, calls=%fused_computation.6 | convolution fusion | flops 50593920 | bytes 4718720 | tf_op jit(solution)/shard_map/ot,tif->oif/dot_general | solution.py:46
  37.0 0.9 copy.13
  38.0 21.4 %reduce-scatter.2.cloned.1.call-done = bf16[128,512]{1,0:T(8,128)(2,1)} async-done(((bf16[512,512]{1,0:T(8,128)(2,1)}), bf16[128,512]{1,0:T(8,128)(2,1)}) %reduce-scatter.2.cloned.1.call-update) | async-done | bytes 131088 | tf_op jit(solution)/shard_map/reduce_scatter | solution.py:47
  59.4 1.1 fusion.38
  60.9 15.9 %all_gather.3 = bf16[512,512]{1,0:T(8,128)(2,1)S(1)} all-gather(bf16[128,512]{1,0:T(8,128)(2,1)S(1)} %convolution_convert_fusion), channel_id=1, replica_groups=mesh['row'=4,'col'=4,'rep'=2] {'col'}, dimensions={0}, use_global_device_ids=true | all-gather | bytes 655360 | tf_op jit(solution)/shard_map/all_gather | solution.py:65
  77.4 2.8 %fusion.10 = f32[16,512,128]{2,1,0:T(8,128)} fusion(bf16[16,128,512]{2,1,0:T(8,128)(2,1)S(1)} %gather_fusion.1, bf16[1,16,128,128]{3,2,1,0:T(8,128)(2,1)S(1)} %copy-done), kind=kOutput, calls=%fused_computation.10 | convolution fusion | flops 268435456 | bytes 6815744 | tf_op jit(solution)/shard_map/tij,tif->tjf/dot_general | solution.py:67
  80.2 5.5 %copy.17 = f32[16,512,128]{1,0,2:T(8,128)} copy(f32[16,512,128]{2,1,0:T(8,128)} %fusion.10) | data formatting | bytes 8388608 | tf_op jit(solution)/shard_map/tij,tif->tjf/dot_general | solution.py:67
  85.7 1.4 fusion.34
  87.1 4.3 %fusion.7 = bf16[4,128,512]{2,0,1:T(4,128)(2,1)S(1)} fusion(f32[16,512,128]{1,0,2:T(8,128)} %copy.17, s32[16]{0:T(128)S(1)} %bitcast.83, f32[16]{0:T(128)S(1)} %compare_convert_fusion), kind=kOutput, calls=%fused_computation.7 | convolution fusion | flops 50593920 | bytes 4718720 | tf_op jit(solution)/shard_map/it,tjf->ijf/dot_general | solution.py:68
  91.4 0.7 fusion.37
  92.1 1.3 collective-permute-start.3
  93.5 1.3 collective-permute-start.4
  94.8 4.6 %collective-permute-start.5 = (bf16[128,512]{1,0:T(8,128)(2,1)S(1)}, bf16[128,512]{1,0:T(8,128)(2,1)S(1)}, u32[]{:S(2)}, u32[]{:S(2)}) collective-permute-start(bf16[128,512]{1,0:T(8,128)(2,1)S(1)} %bitcast.75), channel_id=1, source_target_pairs={{0,8},{8,16},{16,24},{1,9},{9,17},{17,25},{2,10},{10,18},{18,26},{... | collective-permute-start | bytes 393224 | tf_op jit(solution)/shard_map/ppermute | solution.py:12
  99.4 0.7 fusion.19
  100.3 1.7 collective-permute-done.5
  102.7 112.6 %all-reduce.2.cloned.1.call-done = f32[512,512]{1,0:T(8,128)} async-done(((f32[512,512]{1,0:T(8,128)}), f32[512,512]{1,0:T(8,128)}) %all-reduce.2.cloned.1.call-update) | async-done | bytes 1048592 | tf_op jit(solution)/shard_map/psum | solution.py:61
  215.3 2.3 %broadcast_multiply_fusion = f32[512,512]{1,0:T(8,128)} fusion(f32[512,512]{1,0:T(8,128)} %all-reduce.2.cloned.1.call-done), kind=kLoop, calls=%fused_computation.14 | loop fusion | flops 262144 | bytes 2097152 | tf_op jit(solution)/shard_map/mul | solution.py:61
  (32 shorter events, 3.7 us)
Async XLA Ops:
  7.2 17.2 %copy-start = (bf16[1,16,128,128]{3,2,1,0:T(8,128)(2,1)S(1)}, bf16[1,16,128,128]{3,2,1,0:T(8,128)(2,1)}, u32[]{:S(2)}) copy-start(bf16[1,16,128,128]{3,2,1,0:T(8,128)(2,1)} %param.10) | copy-start | bytes 1572868
  7.2 52.2 %reduce-scatter.2.cloned.1.call-start = ((), (), s32[]{:S(2)}) async-start(), calls=%async_computation.1 | async-start | bytes 655360 | tf_op jit(solution)/shard_map/reduce_scatter | solution.py:47
  7.2 11.1 %collective-permute-start = (bf16[128,512]{1,0:T(8,128)(2,1)}, bf16[128,512]{1,0:T(8,128)(2,1)S(1)}, u32[]{:S(2)}, u32[]{:S(2)}) collective-permute-start(bf16[128,512]{1,0:T(8,128)(2,1)} %bitcast.76), channel_id=1, source_target_pairs={{0,16},{8,24},{1,17},{9,25},{2,18},{10,26},{3,19},{11,27},{4,20},{... | collective-permute-start | bytes 393224 | tf_op jit(solution)/shard_map/ppermute | solution.py:12
  12.2 6.2 %collective-permute-start.1 = (bf16[128,512]{1,0:T(8,128)(2,1)}, bf16[128,512]{1,0:T(8,128)(2,1)S(1)}, u32[]{:S(2)}, u32[]{:S(2)}) collective-permute-start(bf16[128,512]{1,0:T(8,128)(2,1)} %bitcast.77), channel_id=1, source_target_pairs={{0,8},{8,16},{16,24},{1,9},{9,17},{17,25},{2,10},{10,18},{18,26},{... | collective-permute-start | bytes 393224 | tf_op jit(solution)/shard_map/ppermute | solution.py:12
  15.7 7.1 %collective-permute-start.2 = (bf16[128,512]{1,0:T(8,128)(2,1)}, bf16[128,512]{1,0:T(8,128)(2,1)S(1)}, u32[]{:S(2)}, u32[]{:S(2)}) collective-permute-start(bf16[128,512]{1,0:T(8,128)(2,1)} %bitcast.78), channel_id=1, source_target_pairs={{8,0},{16,8},{24,16},{9,1},{17,9},{25,17},{10,2},{18,10},{26,18},{... | collective-permute-start | bytes 393224 | tf_op jit(solution)/shard_map/ppermute | solution.py:12
  27.1 5.5 %copy-start.3 = (s32[1,16]{1,0:T(1,128)S(1)}, s32[1,16]{1,0:T(1,128)}, u32[]{:S(2)}) copy-start(s32[1,16]{1,0:T(1,128)} %param.11) | copy-start | bytes 196
  32.6 26.8 %copy-start.1 = (bf16[512,512]{1,0:T(8,128)(2,1)S(1)}, bf16[512,512]{1,0:T(8,128)(2,1)}, u32[]{:S(2)}) copy-start(bf16[512,512]{1,0:T(8,128)(2,1)} %param.9) | copy-start | bytes 1572868
  37.0 23.6 %copy-start.5 = (bf16[1,128,512]{2,1,0:T(8,128)(2,1)S(1)}, bf16[1,128,512]{2,1,0:T(8,128)(2,1)}, u32[]{:S(2)}) copy-start(bf16[1,128,512]{2,1,0:T(8,128)(2,1)} %param.8) | copy-start | bytes 393220
  37.9 177.4 %all-reduce.2.cloned.1.call-start = ((), (), s32[]{:S(2)}) async-start(), calls=%async_computation.2 | async-start | bytes 2097152 | tf_op jit(solution)/shard_map/psum | solution.py:61
  80.2 5.5 %copy-start.2 = (bf16[128,512]{1,0:T(8,128)(2,1)S(1)}, bf16[128,512]{1,0:T(8,128)(2,1)}, u32[]{:S(2)}) copy-start(bf16[128,512]{1,0:T(8,128)(2,1)} %reduce-scatter.2.cloned.1.call-done) | copy-start | bytes 393220
  85.7 1.4 copy-start.4
  92.1 8.0 %collective-permute-start.3 = (bf16[128,512]{1,0:T(8,128)(2,1)S(1)}, bf16[128,512]{1,0:T(8,128)(2,1)S(1)}, u32[]{:S(2)}, u32[]{:S(2)}) collective-permute-start(bf16[128,512]{1,0:T(8,128)(2,1)S(1)} %bitcast.73), channel_id=1, source_target_pairs={{16,0},{24,8},{17,1},{25,9},{18,2},{26,10},{19,3},{27,11},{20,4},{... | collective-permute-start | bytes 393224 | tf_op jit(solution)/shard_map/ppermute | solution.py:12
  93.5 6.9 %collective-permute-start.4 = (bf16[128,512]{1,0:T(8,128)(2,1)S(1)}, bf16[128,512]{1,0:T(8,128)(2,1)S(1)}, u32[]{:S(2)}, u32[]{:S(2)}) collective-permute-start(bf16[128,512]{1,0:T(8,128)(2,1)S(1)} %bitcast.74), channel_id=1, source_target_pairs={{8,0},{16,8},{24,16},{9,1},{17,9},{25,17},{10,2},{18,10},{26,18},{... | collective-permute-start | bytes 393224 | tf_op jit(solution)/shard_map/ppermute | solution.py:12
  94.8 7.2 %collective-permute-start.5 = (bf16[128,512]{1,0:T(8,128)(2,1)S(1)}, bf16[128,512]{1,0:T(8,128)(2,1)S(1)}, u32[]{:S(2)}, u32[]{:S(2)}) collective-permute-start(bf16[128,512]{1,0:T(8,128)(2,1)S(1)} %bitcast.75), channel_id=1, source_target_pairs={{0,8},{8,16},{16,24},{1,9},{9,17},{17,25},{2,10},{10,18},{18,26},{... | collective-permute-start | bytes 393224 | tf_op jit(solution)/shard_map/ppermute | solution.py:12
Sparse Core Ops, SparseCore 0:
  38.0 21.3 reduce-scatter.1
  87.2 128.0 all-reduce.1
where the time goes:
time: 225 us; the launch traced here: 224 us
  waiting for transfers between devices  140 us (62%)
  starting transfers between devices  16.9 us (8%)
  matrix products  16.9 us (8%)
  blocking collectives  15.9 us (7%)
  between operations  14.9 us (7%)
  local copies, waits for them, and re-layouts  13.4 us (6%)
  other arithmetic  6.11 us (3%)
    psum x1, waiting for transfers between devices, body(): lax.psum(local_grad, ('row', 'col', 'rep'))  113 us
    reduce_scatter x1, waiting for transfers between devices, body(): lax.psum_scatter(part.reshape(out_count * edge, width).astype(jnp.bfloat1...  21.4 us
    ppermute x6, starting transfers between devices, passed_along(): lax.ppermute(value, axis, [(source, source + steps) for source in range(l...  16.8 us
    all_gather x1, blocking collectives, body(): lax.all_gather(dhidden, 'col', axis=0, tiled=True)  15.9 us
    ppermute x6, waiting for transfers between devices, passed_along(): lax.ppermute(value, axis, [(source, source + steps) for source in range(l...  6.33 us
    dot_general x1, local copies, waits for them, and re-layouts, body(): jnp.einsum('tij,tif->tjf', values, chosen, preferred_element_type=jnp.flo...  5.54 us
    dot_general x1, local copies, waits for them, and re-layouts, body(): jnp.einsum('tij,tjf->tif', values, picked, preferred_element_type=jnp.flo...  5.51 us
  transfers between devices with their start and end apart: 8, of which 6 were waited for; matrix products, arithmetic and copies ran while one was open for 3% of the time, Pallas kernels for 0%

commit v1 on v0

--- a/solution.py
+++ b/solution.py
@@ -58,7 +58,9 @@
     )
     local_grad = jnp.einsum("nf,ng->fg", summed, dpre, preferred_element_type=jnp.float32)
     total_nodes = node_rows * lax.axis_size("row") * col_count * lax.axis_size("rep")
-    grad_weight = lax.psum(local_grad, ("row", "col", "rep")) * jnp.float32(total_nodes) ** (-0.5)
+    grad_weight = lax.psum(lax.psum(local_grad, ("col", "rep")), "row") * jnp.float32(
+        total_nodes
+    ) ** (-0.5)
     dhidden = jnp.einsum("nf,gf->ng", dpre, weight, preferred_element_type=jnp.float32).astype(
         jnp.bfloat16
     )

time: 225 us -> 190 us (0.84)
  waiting for transfers between devices: 140 us -> 104 us
    psum x1 -> x2, waiting for transfers between devices: 113 us -> 74 us  [the longest x1 41.3 us: body(): lax.psum(lax.psum(local_grad, ('col', 'rep')), 'row')]
    ppermute x6, waiting for transfers between devices: 6.33 us -> 8.58 us  [passed_along(): lax.ppermute(value, axis, [(source, source + steps) for source in range(l...]
  transfers between devices with their start and end apart: 8 -> 9, of which waited for: 6 -> 7; matrix products, arithmetic and copies ran while one was open for 3% -> 9% of each run, Pallas kernels for 0% -> 0%
where the time goes in v1:
time: 190 us; the launch traced here: 189 us
  waiting for transfers between devices  104 us (55%)
  blocking collectives  17.2 us (9%)
  starting transfers between devices  17 us (9%)
  matrix products  16.9 us (9%)
  between operations  14.6 us (8%)
  local copies, waits for them, and re-layouts  13.4 us (7%)
  other arithmetic  6.12 us (3%)
    psum x1, waiting for transfers between devices, body(): lax.psum(lax.psum(local_grad, ('col', 'rep')), 'row')  41.3 us
    psum x1, waiting for transfers between devices, body(): lax.psum(local_grad, ('col', 'rep'))  32.7 us
    reduce_scatter x1, waiting for transfers between devices, body(): lax.psum_scatter(part.reshape(out_count * edge, width).astype(jnp.bfloat1...  21.4 us
    all_gather x1, blocking collectives, body(): lax.all_gather(dhidden, 'col', axis=0, tiled=True)  17.2 us
    ppermute x6, starting transfers between devices, passed_along(): lax.ppermute(value, axis, [(source, source + steps) for source in range(l...  16.8 us
    ppermute x6, waiting for transfers between devices, passed_along(): lax.ppermute(value, axis, [(source, source + steps) for source in range(l...  8.58 us
    dot_general x1, local copies, waits for them, and re-layouts, body(): jnp.einsum('tij,tif->tjf', values, chosen, preferred_element_type=jnp.flo...  5.52 us
    dot_general x1, local copies, waits for them, and re-layouts, body(): jnp.einsum('tij,tjf->tif', values, picked, preferred_element_type=jnp.flo...  5.51 us
  transfers between devices with their start and end apart: 9, of which 7 were waited for; matrix products, arithmetic and copies ran while one was open for 9% of the time, Pallas kernels for 0%

profile of v1, /device:TPU:0, one launch (start us, length us, event | category | flops | bytes accessed | tf_op | source)
XLA Modules:
  0.0 189.2 jit_solution(15324118576987524190)
XLA Ops:
  7.2 5.0 %collective-permute-start = (bf16[128,512]{1,0:T(8,128)(2,1)}, bf16[128,512]{1,0:T(8,128)(2,1)S(1)}, u32[]{:S(2)}, u32[]{:S(2)}) collective-permute-start(bf16[128,512]{1,0:T(8,128)(2,1)} %bitcast.76), channel_id=1, source_target_pairs={{0,16},{8,24},{1,17},{9,25},{2,18},{10,26},{3,19},{11,27},{4,20},{... | collective-permute-start | bytes 393224 | tf_op jit(solution)/shard_map/ppermute | solution.py:12
  12.2 3.4 %collective-permute-start.1 = (bf16[128,512]{1,0:T(8,128)(2,1)}, bf16[128,512]{1,0:T(8,128)(2,1)S(1)}, u32[]{:S(2)}, u32[]{:S(2)}) collective-permute-start(bf16[128,512]{1,0:T(8,128)(2,1)} %bitcast.77), channel_id=1, source_target_pairs={{0,8},{8,16},{16,24},{1,9},{9,17},{17,25},{2,10},{10,18},{18,26},{... | collective-permute-start | bytes 393224 | tf_op jit(solution)/shard_map/ppermute | solution.py:12
  15.7 1.3 collective-permute-start.2
  18.5 4.3 %collective-permute-done.2 = bf16[128,512]{1,0:T(8,128)(2,1)S(1)} collective-permute-done((bf16[128,512]{1,0:T(8,128)(2,1)}, bf16[128,512]{1,0:T(8,128)(2,1)S(1)}, u32[]{:S(2)}, u32[]{:S(2)}) %collective-permute-start.2) | collective-permute-done | bytes 131104 | tf_op jit(solution)/shard_map/ppermute | solution.py:12
  22.7 1.0 pad_maximum_fusion
  24.4 2.7 %fusion.12 = f32[16,512,128]{2,1,0:T(8,128)} fusion(bf16[16,128,512]{2,1,0:T(8,128)(2,1)S(1)} %gather_fusion, bf16[1,16,128,128]{3,2,1,0:T(8,128)(2,1)S(1)} %copy-done), kind=kOutput, calls=%fused_computation.12 | convolution fusion | flops 268435456 | bytes 6815744 | tf_op jit(solution)/shard_map/tij,tjf->tif/dot_general | solution.py:45
  27.1 5.5 %copy.16 = f32[16,512,128]{1,0,2:T(8,128)} copy(f32[16,512,128]{2,1,0:T(8,128)} %fusion.12) | data formatting | bytes 8388608 | tf_op jit(solution)/shard_map/tij,tjf->tif/dot_general | solution.py:45
  32.6 4.3 %fusion.4 = bf16[4,128,512]{2,0,1:T(4,128)(2,1)S(1)} fusion(f32[16,512,128]{1,0,2:T(8,128)} %copy.16, f32[16]{0:T(128)S(1)} %compare_convert_fusion, s32[16]{0:T(128)S(1)} %bitcast.82), kind=kOutput, calls=%fused_computation.6 | convolution fusion | flops 50593920 | bytes 4718720 | tf_op jit(solution)/shard_map/ot,tif->oif/dot_general | solution.py:46
  37.0 0.9 copy.13
  38.0 21.4 %reduce-scatter.2.cloned.1.call-done = bf16[128,512]{1,0:T(8,128)(2,1)} async-done(((bf16[512,512]{1,0:T(8,128)(2,1)}), bf16[128,512]{1,0:T(8,128)(2,1)}) %reduce-scatter.2.cloned.1.call-update) | async-done | bytes 131088 | tf_op jit(solution)/shard_map/reduce_scatter | solution.py:47
  59.4 1.2 fusion.38
  61.0 1.3 fusion.34
  62.4 17.2 %all_gather.3 = bf16[512,512]{1,0:T(8,128)(2,1)S(1)} all-gather(bf16[128,512]{1,0:T(8,128)(2,1)S(1)} %convolution_convert_fusion), channel_id=1, replica_groups=mesh['row'=4,'col'=4,'rep'=2] {'col'}, dimensions={0}, use_global_device_ids=true | all-gather | bytes 655360 | tf_op jit(solution)/shard_map/all_gather | solution.py:67
  80.3 2.8 %fusion.10 = f32[16,512,128]{2,1,0:T(8,128)} fusion(bf16[16,128,512]{2,1,0:T(8,128)(2,1)S(1)} %gather_fusion.1, bf16[1,16,128,128]{3,2,1,0:T(8,128)(2,1)S(1)} %copy-done), kind=kOutput, calls=%fused_computation.10 | convolution fusion | flops 268435456 | bytes 6815744 | tf_op jit(solution)/shard_map/tij,tif->tjf/dot_general | solution.py:69
  83.0 5.5 %copy.17 = f32[16,512,128]{1,0,2:T(8,128)} copy(f32[16,512,128]{2,1,0:T(8,128)} %fusion.10) | data formatting | bytes 8388608 | tf_op jit(solution)/shard_map/tij,tif->tjf/dot_general | solution.py:69
  88.5 32.7 %all-reduce.3.cloned.1.call-done = f32[512,512]{1,0:T(8,128)} async-done(((f32[512,512]{1,0:T(8,128)}), f32[512,512]{1,0:T(8,128)}) %all-reduce.3.cloned.1.call-update) | async-done | bytes 1048592 | tf_op jit(solution)/shard_map/psum | solution.py:61
  121.3 4.3 %fusion.7 = bf16[4,128,512]{2,0,1:T(4,128)(2,1)S(1)} fusion(f32[16,512,128]{1,0,2:T(8,128)} %copy.17, s32[16]{0:T(128)S(1)} %bitcast.83, f32[16]{0:T(128)S(1)} %compare_convert_fusion), kind=kOutput, calls=%fused_computation.7 | convolution fusion | flops 50593920 | bytes 4718720 | tf_op jit(solution)/shard_map/it,tjf->ijf/dot_general | solution.py:70
  126.3 1.3 collective-permute-start.3
  127.7 1.3 collective-permute-start.4
  129.0 4.6 %collective-permute-start.5 = (bf16[128,512]{1,0:T(8,128)(2,1)S(1)}, bf16[128,512]{1,0:T(8,128)(2,1)S(1)}, u32[]{:S(2)}, u32[]{:S(2)}) collective-permute-start(bf16[128,512]{1,0:T(8,128)(2,1)S(1)} %bitcast.75), channel_id=1, source_target_pairs={{0,8},{8,16},{16,24},{1,9},{9,17},{17,25},{2,10},{10,18},{18,26},{... | collective-permute-start | bytes 393224 | tf_op jit(solution)/shard_map/ppermute | solution.py:12
  134.3 1.4 collective-permute-done.3
  135.7 2.7 %collective-permute-done.4 = bf16[128,512]{1,0:T(8,128)(2,1)S(1)} collective-permute-done((bf16[128,512]{1,0:T(8,128)(2,1)S(1)}, bf16[128,512]{1,0:T(8,128)(2,1)S(1)}, u32[]{:S(2)}, u32[]{:S(2)}) %collective-permute-start.4) | collective-permute-done | bytes 131104 | tf_op jit(solution)/shard_map/ppermute | solution.py:12
  139.2 41.3 %all-reduce.5.cloned.1.call-done = f32[512,512]{1,0:T(8,128)} async-done(((f32[512,512]{1,0:T(8,128)}), f32[512,512]{1,0:T(8,128)}) %all-reduce.5.cloned.1.call-update) | async-done | bytes 1048592 | tf_op jit(solution)/shard_map/psum | solution.py:61
  180.4 2.3 %broadcast_multiply_fusion = f32[512,512]{1,0:T(8,128)} fusion(f32[512,512]{1,0:T(8,128)} %all-reduce.5.cloned.1.call-done), kind=kLoop, calls=%fused_computation.14 | loop fusion | flops 262144 | bytes 2097152 | tf_op jit(solution)/shard_map/mul | solution.py:61
  (35 shorter events, 5.0 us)
Async XLA Ops:
  7.2 17.2 %copy-start = (bf16[1,16,128,128]{3,2,1,0:T(8,128)(2,1)S(1)}, bf16[1,16,128,128]{3,2,1,0:T(8,128)(2,1)}, u32[]{:S(2)}) copy-start(bf16[1,16,128,128]{3,2,1,0:T(8,128)(2,1)} %param.10) | copy-start | bytes 1572868
  7.2 52.2 %reduce-scatter.2.cloned.1.call-start = ((), (), s32[]{:S(2)}) async-start(), calls=%async_computation.1 | async-start | bytes 655360 | tf_op jit(solution)/shard_map/reduce_scatter | solution.py:47
  7.2 11.1 %collective-permute-start = (bf16[128,512]{1,0:T(8,128)(2,1)}, bf16[128,512]{1,0:T(8,128)(2,1)S(1)}, u32[]{:S(2)}, u32[]{:S(2)}) collective-permute-start(bf16[128,512]{1,0:T(8,128)(2,1)} %bitcast.76), channel_id=1, source_target_pairs={{0,16},{8,24},{1,17},{9,25},{2,18},{10,26},{3,19},{11,27},{4,20},{... | collective-permute-start | bytes 393224 | tf_op jit(solution)/shard_map/ppermute | solution.py:12
  12.2 6.2 %collective-permute-start.1 = (bf16[128,512]{1,0:T(8,128)(2,1)}, bf16[128,512]{1,0:T(8,128)(2,1)S(1)}, u32[]{:S(2)}, u32[]{:S(2)}) collective-permute-start(bf16[128,512]{1,0:T(8,128)(2,1)} %bitcast.77), channel_id=1, source_target_pairs={{0,8},{8,16},{16,24},{1,9},{9,17},{17,25},{2,10},{10,18},{18,26},{... | collective-permute-start | bytes 393224 | tf_op jit(solution)/shard_map/ppermute | solution.py:12
  15.7 7.1 %collective-permute-start.2 = (bf16[128,512]{1,0:T(8,128)(2,1)}, bf16[128,512]{1,0:T(8,128)(2,1)S(1)}, u32[]{:S(2)}, u32[]{:S(2)}) collective-permute-start(bf16[128,512]{1,0:T(8,128)(2,1)} %bitcast.78), channel_id=1, source_target_pairs={{8,0},{16,8},{24,16},{9,1},{17,9},{25,17},{10,2},{18,10},{26,18},{... | collective-permute-start | bytes 393224 | tf_op jit(solution)/shard_map/ppermute | solution.py:12
  27.1 5.5 %copy-start.3 = (s32[1,16]{1,0:T(1,128)S(1)}, s32[1,16]{1,0:T(1,128)}, u32[]{:S(2)}) copy-start(s32[1,16]{1,0:T(1,128)} %param.11) | copy-start | bytes 196
  32.6 26.8 %copy-start.1 = (bf16[512,512]{1,0:T(8,128)(2,1)S(1)}, bf16[512,512]{1,0:T(8,128)(2,1)}, u32[]{:S(2)}) copy-start(bf16[512,512]{1,0:T(8,128)(2,1)} %param.9) | copy-start | bytes 1572868
  37.0 23.6 %copy-start.5 = (bf16[1,128,512]{2,1,0:T(8,128)(2,1)S(1)}, bf16[1,128,512]{2,1,0:T(8,128)(2,1)}, u32[]{:S(2)}) copy-start(bf16[1,128,512]{2,1,0:T(8,128)(2,1)} %param.8) | copy-start | bytes 393220
  37.9 83.3 %all-reduce.3.cloned.1.call-start = ((), (), s32[]{:S(2)}) async-start(), calls=%async_computation.2 | async-start | bytes 2097152 | tf_op jit(solution)/shard_map/psum | solution.py:61
  59.4 1.5 copy-start.2
  62.3 118.1 %all-reduce.5.cloned.1.call-start = ((), (), s32[]{:S(2)}) async-start(), calls=%async_computation.3 | async-start | bytes 2097152 | tf_op jit(solution)/shard_map/psum | solution.py:61
  83.0 38.3 %copy-start.4 = (s32[1,16]{1,0:T(1,128)S(1)}, s32[1,16]{1,0:T(1,128)}, u32[]{:S(2)}) copy-start(s32[1,16]{1,0:T(1,128)} %param.12) | copy-start | bytes 196
  126.3 9.4 %collective-permute-start.3 = (bf16[128,512]{1,0:T(8,128)(2,1)S(1)}, bf16[128,512]{1,0:T(8,128)(2,1)S(1)}, u32[]{:S(2)}, u32[]{:S(2)}) collective-permute-start(bf16[128,512]{1,0:T(8,128)(2,1)S(1)} %bitcast.73), channel_id=1, source_target_pairs={{16,0},{24,8},{17,1},{25,9},{18,2},{26,10},{19,3},{27,11},{20,4},{... | collective-permute-start | bytes 393224 | tf_op jit(solution)/shard_map/ppermute | solution.py:12
  127.7 10.8 %collective-permute-start.4 = (bf16[128,512]{1,0:T(8,128)(2,1)S(1)}, bf16[128,512]{1,0:T(8,128)(2,1)S(1)}, u32[]{:S(2)}, u32[]{:S(2)}) collective-permute-start(bf16[128,512]{1,0:T(8,128)(2,1)S(1)} %bitcast.74), channel_id=1, source_target_pairs={{8,0},{16,8},{24,16},{9,1},{17,9},{25,17},{10,2},{18,10},{26,18},{... | collective-permute-start | bytes 393224 | tf_op jit(solution)/shard_map/ppermute | solution.py:12
  129.0 9.5 %collective-permute-start.5 = (bf16[128,512]{1,0:T(8,128)(2,1)S(1)}, bf16[128,512]{1,0:T(8,128)(2,1)S(1)}, u32[]{:S(2)}, u32[]{:S(2)}) collective-permute-start(bf16[128,512]{1,0:T(8,128)(2,1)S(1)} %bitcast.75), channel_id=1, source_target_pairs={{0,8},{8,16},{16,24},{1,9},{9,17},{17,25},{2,10},{10,18},{18,26},{... | collective-permute-start | bytes 393224 | tf_op jit(solution)/shard_map/ppermute | solution.py:12
Sparse Core Ops, SparseCore 0:
  38.0 21.3 reduce-scatter.1
  62.4 58.7 all-reduce.2
  124.3 56.0 all-reduce.4
